TPU v7x, 32 devices: a whole 2x2x4 slice. The times are simulated.
32 devices in a mesh: groups: 2 (over y), gx: 2 (over core), gy: 8 (over z, x).
Axes of the slice: x: 2, y: 2, z: 4, core: 2. Of those that a mesh axis runs over, the one named last changes fastest.
Arguments:
- tokens: bfloat16 [512, 8192], P(('groups', 'gy'), 'gx'), parts along dimension 0, may hold values from -6 to 6
- gate_weight: bfloat16 [8192, 26624], P('gx', 'gy'), may hold values from -0.0625 to 0.0625
- up_weight: bfloat16 [8192, 26624], P('gx', 'gy'), may hold values from -0.0625 to 0.0625
- down_weight: bfloat16 [26624, 8192], P('gy', 'gx'), may hold values from -0.0546875 to 0.0546875
Outputs:
- mixed: bfloat16 [512, 8192], P(('groups', 'gy'), 'gx'), parts along dimension 0
There are 2 independent parts, one for each index of `groups`. A program takes and returns all parts, laid end to end along the dimension named above; an argument that names none is the same for every part. Nothing has to cross between parts.
All inputs are finite; a program needn't handle non-finite values.
Results may differ from a plain program's by a relative error of at most 0.0049.
Values may be sent and summed in bfloat16 or wider, within the bound.
A program may use at most 192 MiB of HBM per device.

v0:
```python
import jax
import jax.numpy as jnp
from jax import lax
from jax.sharding import PartitionSpec as P


def local(tokens, gate_weight, up_weight, down_weight):
    piece = lax.all_gather(tokens, "gy", axis=0, tiled=True)
    gate_part = jnp.dot(piece, gate_weight, preferred_element_type=jnp.float32)
    up_part = jnp.dot(piece, up_weight, preferred_element_type=jnp.float32)
    gate, up = lax.psum((gate_part, up_part), "gx")
    hidden = (jax.nn.silu(gate) * up).astype(jnp.bfloat16)
    summed = lax.psum_scatter(
        jnp.dot(hidden, down_weight, preferred_element_type=jnp.float32),
        "gy",
        scatter_dimension=0,
        tiled=True,
    )
    return summed.astype(jnp.bfloat16)


def solution(mesh):
    placed = (P(("groups", "gy"), "gx"), P("gx", "gy"), P("gx", "gy"), P("gy", "gx"))
    return jax.shard_map(
        local, mesh=mesh, in_specs=placed, out_specs=P(("groups", "gy"), "gx"), check_vma=False
    )
```

profile of v0, /device:TPU:0, one launch (start us, length us, event | category | flops | bytes accessed | tf_op | source)
XLA Modules:
  0.0 239.5 jit_solution(13195979652174822006)
XLA Ops:
  6.5 0.0 all-gather.2.cloned.1.call-start
  6.5 0.7 all-gather.2.cloned.1.call-update
  7.3 0.0 all-reduce.3.cloned.1.call-start
  7.3 54.2 %all-gather.2.cloned.1.call-done = bf16[256,4096]{1,0:T(8,128)(2,1)} async-done(((bf16[32,4096]{1,0:T(8,128)(2,1)}), bf16[256,4096]{1,0:T(8,128)(2,1)}) %all-gather.2.cloned.1.call-update) | async-done | bytes 2097168 | tf_op jit(solution)/shard_map/all_gather | solution.py:8
  61.5 0.0 copy-start
  61.5 18.6 %fusion.4 = f32[256,3328]{1,0:T(8,128)} fusion(bf16[256,4096]{1,0:T(8,128)(2,1)} %all-gather.2.cloned.1.call-done, bf16[4096,3328]{1,0:T(8,128)(2,1)} %param.6), kind=kOutput, calls=%fused_computation.5 | convolution fusion | flops 6979321856 | bytes 32768000 | tf_op jit(solution)/shard_map/dot_general | solution.py:10
  80.1 0.0 copy-done
  80.1 14.3 %fusion.3 = f32[256,3328]{1,0:T(8,128)} fusion(bf16[256,4096]{1,0:T(8,128)(2,1)S(1)} %copy-done, bf16[4096,3328]{1,0:T(8,128)(2,1)} %param.5), kind=kOutput, calls=%fused_computation.4 | convolution fusion | flops 6979321856 | bytes 32768000 | tf_op jit(solution)/shard_map/dot_general | solution.py:9
  94.4 0.0 all-reduce.3.cloned.1.call-update
  94.4 0.0 reduce-scatter.2.cloned.1.call-start
  94.5 31.6 %all-reduce.3.cloned.1.call-done = (f32[256,3328]{1,0:T(8,128)}, f32[256,3328]{1,0:T(8,128)}) async-done(((f32[256,3328]{1,0:T(8,128)}, f32[256,3328]{1,0:T(8,128)}), (f32[256,3328]{1,0:T(8,128)}, f32[256,3328]{1,0:T(8,128)})) %all-reduce.3.cloned.1.call-update) | async-done | bytes 6815760 | tf_op jit(solution)/shard_map/psum | solution.py:11
  126.1 15.9 %fusion = f32[256,4096]{1,0:T(8,128)} fusion(bf16[3328,4096]{1,0:T(8,128)(2,1)} %param.7, f32[256,3328]{1,0:T(8,128)} %get-tuple-element.5, f32[256,3328]{1,0:T(8,128)} %get-tuple-element.6), kind=kOutput, calls=%fused_computation.1 | convolution fusion | flops 6984433664 | bytes 38273024 | tf_op jit(solution)/shard_map/dot_general | solution.py:14
  142.0 0.0 reduce-scatter.2.cloned.1.call-update
  142.0 89.2 %reduce-scatter.2.cloned.1.call-done = f32[32,4096]{1,0:T(8,128)} async-done(((f32[256,4096]{1,0:T(8,128)}), f32[32,4096]{1,0:T(8,128)}) %reduce-scatter.2.cloned.1.call-update) | async-done | bytes 524304 | tf_op jit(solution)/shard_map/reduce_scatter | solution.py:13
  231.2 1.8 convert_element_type.7
Async XLA Ops:
  6.5 55.0 %all-gather.2.cloned.1.call-start = ((), (), s32[]{:S(2)}) async-start(), calls=%async_computation.1 | async-start | bytes 2359296 | tf_op jit(solution)/shard_map/all_gather | solution.py:8
  7.3 118.8 %all-reduce.3.cloned.1.call-start = ((), (), s32[]{:S(2)}) async-start(), calls=%async_computation.3 | async-start | bytes 13631488 | tf_op jit(solution)/shard_map/psum | solution.py:11
  61.5 18.6 %copy-start = (bf16[256,4096]{1,0:T(8,128)(2,1)S(1)}, bf16[256,4096]{1,0:T(8,128)(2,1)}, u32[]{:S(2)}) copy-start(bf16[256,4096]{1,0:T(8,128)(2,1)} %all-gather.2.cloned.1.call-done) | copy-start | bytes 6291460
  94.4 136.8 %reduce-scatter.2.cloned.1.call-start = ((), (), s32[]{:S(2)}) async-start(), calls=%async_computation.2 | async-start | bytes 4718592 | tf_op jit(solution)/shard_map/reduce_scatter | solution.py:13
Sparse Core Ops, SparseCore 0:
  9.5 51.9 all-gather.1
  94.5 31.5 all-reduce.2
  142.1 89.0 reduce-scatter.1
where the time goes:
time: 240 us
  waiting for transfers between devices  176 us (73%)
  matrix products  48.8 us (20%)
  between operations  13.1 us (5%)
    reduce_scatter x1, waiting for transfers between devices, local(): lax.psum_scatter(jnp.dot(hidden, down_weight, preferred_element_type=jnp....  89.2 us
    all_gather x1, waiting for transfers between devices, local(): piece = lax.all_gather(tokens, 'gy', axis=0, tiled=True)  54.2 us
    psum x1, waiting for transfers between devices, local(): gate, up = lax.psum((gate_part, up_part), 'gx')  31.6 us
    dot_general x1, matrix products, local(): up_part = jnp.dot(piece, up_weight, preferred_element_type=jnp.float32)  18.6 us
    dot_general x1, matrix products, local(): jnp.dot(hidden, down_weight, preferred_element_type=jnp.float32)  15.9 us
    dot_general x1, matrix products, local(): gate_part = jnp.dot(piece, gate_weight, preferred_element_type=jnp.float32)  14.3 us
  transfers between devices with their start and end apart: 3, of which 3 were waited for; matrix products, arithmetic and copies ran while one was open for 0% of the time, Pallas kernels for 0%

commit v1 on v0

v1 whole, which is shorter than its diff:
```python
import functools

import jax
import jax.numpy as jnp
from jax import lax
from jax.experimental import pallas as pl
from jax.experimental.pallas import tpu as pltpu
from jax.sharding import PartitionSpec as P

F32, BF16 = jnp.float32, jnp.bfloat16
MESH = pl.DeviceIdType.MESH
CW = 256
RING = 10
KEEP = 4
LAG = 2
CUT = 2
EX = F32


def local(tokens, gate_weight, up_weight, down_weight):
    piece = lax.all_gather(tokens, "gy", axis=0, tiled=True)
    gate_part = jnp.dot(piece, gate_weight, preferred_element_type=F32)
    up_part = jnp.dot(piece, up_weight, preferred_element_type=F32)
    gate, up = lax.psum((gate_part, up_part), "gx")
    hidden = (jax.nn.silu(gate) * up).astype(BF16)
    summed = lax.psum_scatter(
        jnp.dot(hidden, down_weight, preferred_element_type=F32), "gy", scatter_dimension=0, tiled=True
    )
    return summed.astype(BF16)


def kernel(rows, width, units, nz,
           tok, gw, uw, dw, out,
           ring, x_all, hid, part, precv, yown, xsend, xrecv, zsend, zrecv, fin,
           ring_sem, own_sem, up_send, dn_send, line_recv, xf_send, xf_recv,
           part_send, part_recv, hid_send, hid_recv, xs_send, xs_recv, zs_send, zs_recv):
    gx = lax.axis_index("gx")
    gy = lax.axis_index("gy")
    z, x = gy // 2, gy % 2
    line = nz * rows
    half = line
    chunks, groups = units // CW, width // (2 * CW)
    core = {"gx": 1 - gx}
    across = {"gy": z * 2 + 1 - x}

    def along(zz):
        return {"gy": zz * 2 + x}

    def gu_copy(c, which):
        src = (gw, uw)[which].at[:, pl.ds(pl.multiple_of(c * CW, CW), CW)]
        s = c % RING
        return pltpu.make_async_copy(src, ring.at[s, which], ring_sem.at[s, which])

    def d_copy(g, which):
        src = dw.at[:, pl.ds(pl.multiple_of((g * 2 + which) * CW, CW), CW)]
        s = (chunks + g) % RING
        return pltpu.make_async_copy(src, ring.at[s, which, pl.ds(0, units)], ring_sem.at[s, which])

    for c in range(min(RING, chunks)):
        gu_copy(c, 0).start()
        gu_copy(c, 1).start()

    barrier = pltpu.get_barrier_semaphore()
    pl.semaphore_signal(barrier, inc=1, device_id=core, device_id_type=MESH)
    pl.semaphore_signal(barrier, inc=1, device_id=across, device_id_type=MESH)
    for k in range(1, nz):
        pl.semaphore_signal(barrier, inc=1, device_id=along(lax.rem(z + k, nz)), device_id_type=MESH)
    pl.semaphore_wait(barrier, nz + 1)

    cut = rows // CUT

    def place(block, h, far):
        return x_all.at[pl.ds(pl.multiple_of(far * line + block * rows + h * cut, cut), cut)]

    def source(block, h, own):
        return tok.at[pl.ds(h * cut, cut)] if own else place(block, h, 0)

    def line_copy(block, h, own, step, sems):
        return pltpu.make_async_remote_copy(
            src_ref=source(block, h, own), dst_ref=place(block, h, 0),
            send_sem=sems.at[block, h], recv_sem=line_recv.at[block, h],
            device_id=along(z + step), device_id_type=MESH)

    def cross_copy(block, h, own):
        return pltpu.make_async_remote_copy(
            src_ref=source(block, h, own), dst_ref=place(block, h, 1),
            send_sem=xf_send.at[block, h], recv_sem=xf_recv.at[block, h],
            device_id=across, device_id_type=MESH)

    for h in range(CUT):
        @pl.when(z < nz - 1)
        def _():
            line_copy(z, h, True, 1, up_send).start()

        @pl.when(z > 0)
        def _():
            line_copy(z, h, True, -1, dn_send).start()

        cross_copy(z, h, True).start()
    keep = pltpu.make_async_copy(tok, x_all.at[pl.ds(pl.multiple_of(z * rows, rows), rows)], own_sem)
    keep.start()
    for t in range(1, nz):
        for h in range(CUT):
            @pl.when(z - t >= 0)
            def _():
                line_copy(z - t, h, False, 1, up_send).wait_recv()

                @pl.when(z < nz - 1)
                def _():
                    line_copy(z - t, h, False, 1, up_send).start()

                cross_copy(z - t, h, False).start()

            @pl.when(z + t < nz)
            def _():
                line_copy(z + t, h, False, -1, dn_send).wait_recv()

                @pl.when(z > 0)
                def _():
                    line_copy(z + t, h, False, -1, dn_send).start()

                cross_copy(z + t, h, False).start()
    keep.wait()
    for b in range(nz):
        for h in range(CUT):
            cross_copy(b, h, False).wait_recv()

    def part_copy(c):
        return pltpu.make_async_remote_copy(
            src_ref=part.at[c % KEEP, 1 - gx], dst_ref=precv.at[c],
            send_sem=part_send.at[c % KEEP], recv_sem=part_recv.at[c],
            device_id=core, device_id_type=MESH)

    def hid_at(c, which):
        return hid.at[pl.ds(pl.multiple_of(which * half, half), half), pl.ds(pl.multiple_of(c * CW, CW), CW)]

    def hid_copy(c, which):
        return pltpu.make_async_remote_copy(
            src_ref=hid_at(c, which), dst_ref=hid_at(c, which),
            send_sem=hid_send.at[c], recv_sem=hid_recv.at[c],
            device_id=core, device_id_type=MESH)

    def finish(c):
        part_copy(c).wait_recv()
        gate = part[c % KEEP, gx, 0].astype(F32) + precv[c, 0].astype(F32)
        up = part[c % KEEP, gx, 1].astype(F32) + precv[c, 1].astype(F32)
        hid_at(c, gx)[...] = (gate / (1.0 + jnp.exp(-gate)) * up).astype(BF16)
        hid_copy(c, gx).start()

    def gu_step(c, carry):
        s = c % RING

        @pl.when(c >= KEEP)
        def _():
            part_copy(c - KEEP).wait_send()

        for which in range(2):
            gu_copy(c, which).wait()
            term = jnp.dot(x_all[...], ring[s, which], preferred_element_type=F32)
            part[c % KEEP, 0, which] = term[:half].astype(part.dtype)
            part[c % KEEP, 1, which] = term[half:].astype(part.dtype)
        part_copy(c).start()
        nxt = c + RING

        @pl.when(nxt < chunks)
        def _():
            gu_copy(nxt, 0).start()
            gu_copy(nxt, 1).start()

        @pl.when((nxt >= chunks) & (nxt < chunks + groups))
        def _():
            d_copy(nxt - chunks, 0).start()
            d_copy(nxt - chunks, 1).start()

        @pl.when(c >= 1)
        def _():
            finish(c - 1)
        return carry

    lax.fori_loop(0, chunks, gu_step, 0)
    finish(chunks - 1)
    for c in range(chunks):
        hid_copy(c, 1 - gx).wait_recv()

    def x_copy(g):
        return pltpu.make_async_remote_copy(
            src_ref=xsend.at[g], dst_ref=xrecv.at[g], send_sem=xs_send.at[g], recv_sem=xs_recv.at[g],
            device_id=across, device_id_type=MESH)

    def z_copy(g, k):
        return pltpu.make_async_remote_copy(
            src_ref=zsend.at[k - 1, g], dst_ref=zrecv.at[k - 1, g],
            send_sem=zs_send.at[k - 1, g], recv_sem=zs_recv.at[k - 1, g],
            device_id=along(lax.rem(z + k, nz)), device_id_type=MESH)

    def pair(g):
        x_copy(g).wait_recv()
        for k in range(nz):
            at = pl.ds(pl.multiple_of(lax.rem(z + k, nz) * rows, rows), rows)
            both = yown[g, :, at, :] + xrecv[g, :, at, :].astype(F32)
            if k == 0:
                fin[g] = both
            else:
                zsend[k - 1, g] = both.astype(BF16)
                z_copy(g, k).start()

    def d_step(g, carry):
        s = (chunks + g) % RING
        for which in range(2):
            d_copy(g, which).wait()
            y = jnp.dot(hid[...], ring[s, which, :units], preferred_element_type=F32)
            yown[g, which] = y[:line]
            xsend[g, which] = y[line:].astype(BF16)
        x_copy(g).start()

        @pl.when(g >= LAG)
        def _():
            pair(g - LAG)
        return carry

    lax.fori_loop(0, groups, d_step, 0)
    for g in range(groups - LAG, groups):
        pair(g)
    for g in range(groups):
        total = fin[g]
        for k in range(1, nz):
            z_copy(g, k).wait_recv()
            total = total + zrecv[k - 1, g].astype(F32)
        for which in range(2):
            out[:, pl.ds((g * 2 + which) * CW, CW)] = total[which].astype(BF16)

    for h in range(CUT):
        for b in range(nz):
            cross_copy(b, h, False).wait_send()

            @pl.when((z < nz - 1) & (b <= z))
            def _():
                line_copy(b, h, False, 1, up_send).wait_send()

            @pl.when((z > 0) & (b >= z))
            def _():
                line_copy(b, h, False, -1, dn_send).wait_send()
    for c in range(max(chunks - KEEP, 0), chunks):
        part_copy(c).wait_send()
    for c in range(chunks):
        hid_copy(c, gx).wait_send()
    for g in range(groups):
        x_copy(g).wait_send()
        for k in range(1, nz):
            z_copy(g, k).wait_send()


def fused(nz, tokens, gate_weight, up_weight, down_weight):
    rows, depth = tokens.shape
    units, width = down_weight.shape
    line = nz * rows
    chunks, groups = units // CW, width // (2 * CW)
    dma = pltpu.SemaphoreType.DMA
    flops = 2 * 2 * line * units * (2 * depth + width)
    return pl.pallas_call(
        functools.partial(kernel, rows, width, units, nz),
        out_shape=jax.ShapeDtypeStruct((rows, width), BF16),
        in_specs=[pl.BlockSpec(memory_space=pl.ANY)] * 4,
        out_specs=pl.BlockSpec(memory_space=pltpu.VMEM),
        scratch_shapes=[
            pltpu.VMEM((RING, 2, depth, CW), BF16),
            pltpu.VMEM((2 * line, depth), BF16),
            pltpu.VMEM((2 * line, units), BF16),
            pltpu.VMEM((KEEP, 2, 2, line, CW), EX),
            pltpu.VMEM((chunks, 2, line, CW), EX),
            pltpu.VMEM((groups, 2, line, CW), F32),
            pltpu.VMEM((groups, 2, line, CW), BF16),
            pltpu.VMEM((groups, 2, line, CW), BF16),
            pltpu.VMEM((nz - 1, groups, 2, rows, CW), BF16),
            pltpu.VMEM((nz - 1, groups, 2, rows, CW), BF16),
            pltpu.VMEM((groups, 2, rows, CW), F32),
            dma((RING, 2)),
            dma,
            dma((nz, CUT)),
            dma((nz, CUT)),
            dma((nz, CUT)),
            dma((nz, CUT)),
            dma((nz, CUT)),
            dma((KEEP,)),
            dma((chunks,)),
            dma((chunks,)),
            dma((chunks,)),
            dma((groups,)),
            dma((groups,)),
            dma((nz - 1, groups)),
            dma((nz - 1, groups)),
        ],
        compiler_params=pltpu.CompilerParams(
            collective_id=0, has_side_effects=True, vmem_limit_bytes=60 * 2**20
        ),
        cost_estimate=pl.CostEstimate(
            flops=flops, bytes_accessed=2 * units * (2 * depth + width), transcendentals=line * units
        ),
    )(tokens, gate_weight, up_weight, down_weight)


def solution(mesh):
    placed = (P(("groups", "gy"), "gx"), P("gx", "gy"), P("gx", "gy"), P("gy", "gx"))
    gy, gx = mesh.shape["gy"], mesh.shape["gx"]

    def run(tokens, gate_weight, up_weight, down_weight):
        rows, depth = tokens.shape
        units, width = down_weight.shape
        fits = gy == 8 and gx == 2 and rows == 32 and units % CW == 0 and width % (2 * CW) == 0
        fits = fits and units <= depth == width <= 4096
        fits = fits and RING >= width // (2 * CW) and units // CW >= KEEP
        fits = fits and RING <= units // CW and units <= 3328
        if fits:
            return fused(gy // 2, tokens, gate_weight, up_weight, down_weight)
        return local(tokens, gate_weight, up_weight, down_weight)

    return jax.shard_map(
        run, mesh=mesh, in_specs=placed, out_specs=P(("groups", "gy"), "gx"), check_vma=False
    )
```

time: 240 us -> 98.3 us (0.41)
  waiting for transfers between devices: 176 us -> 0 us
  Pallas kernels: 0 us -> 96.5 us
  matrix products: 48.8 us -> 0 us
  between operations: 13.1 us -> 0.01 us
    pallas_call x0 -> x1, Pallas kernels: none -> 96.5 us  [fused(): pl.pallas_call(functools.partial(kernel, rows, width, units, nz), out_sha...]
    reduce_scatter x1 -> x0, waiting for transfers between devices: 89.2 us -> none  [local(): lax.psum_scatter(jnp.dot(hidden, down_weight, preferred_element_type=jnp....]
    all_gather x1 -> x0, waiting for transfers between devices: 54.2 us -> none  [local(): piece = lax.all_gather(tokens, 'gy', axis=0, tiled=True)]
    dot_general x3 -> x0, matrix products: 48.8 us -> none  [the longest x1 18.6 us: local(): up_part = jnp.dot(piece, up_weight, preferred_element_type=jnp.float32)]
    psum x1 -> x0, waiting for transfers between devices: 31.6 us -> none  [local(): gate, up = lax.psum((gate_part, up_part), 'gx')]
  transfers between devices with their start and end apart: 3 -> 0, of which waited for: 3 -> 0; matrix products, arithmetic and copies ran while one was open for 0% -> 0% of each run, Pallas kernels for 0% -> 0%
where the time goes in v1:
time: 98.3 us; the launch traced here: 98.2 us
  Pallas kernels  96.5 us (98%)
  local copies, waits for them, and re-layouts  1.67 us (2%)
    pallas_call x1, Pallas kernels, fused(): pl.pallas_call(functools.partial(kernel, rows, width, units, nz), out_sha...  96.5 us

profile of v1, /device:TPU:0, one launch (start us, length us, event | category | flops | bytes accessed | tf_op | source)
XLA Modules:
  0.0 98.2 jit_solution(13301483661293029165)
XLA Ops:
  0.0 96.5 %shard_map.46 = bf16[32,4096]{1,0:T(8,128)(2,1)} custom-call(bf16[32,4096]{1,0:T(8,128)(2,1)} %tok.1, bf16[4096,3328]{1,0:T(8,128)(2,1)} %gw.1, bf16[4096,3328]{1,0:T(8,128)(2,1)} %uw.1, bf16[3328,4096]{1,0:T(8,128)(2,1)} %dw.1), custom_call_target="tpu_custom_call" | custom-call | flops 20937965568 | bytes 81788928 | tf_op jit(solution)/shard_map/pallas_call | solution.py:260
  96.5 1.7 %copy.6 = bf16[32,4096]{1,0:T(8,128)(2,1)} copy(bf16[32,4096]{1,0:T(8,128)(2,1)} %shard_map.46) | data formatting | bytes 524288

commit v2 on v1

--- a/solution.py
+++ b/solution.py
@@ -14,7 +14,6 @@
 KEEP = 4
 LAG = 2
 CUT = 2
-EX = F32
 
 
 def local(tokens, gate_weight, up_weight, down_weight):
@@ -38,7 +37,7 @@
     gy = lax.axis_index("gy")
     z, x = gy // 2, gy % 2
     line = nz * rows
-    half = line
+    half = line // 2
     chunks, groups = units // CW, width // (2 * CW)
     core = {"gx": 1 - gx}
     across = {"gy": z * 2 + 1 - x}
@@ -49,12 +48,12 @@
     def gu_copy(c, which):
         src = (gw, uw)[which].at[:, pl.ds(pl.multiple_of(c * CW, CW), CW)]
         s = c % RING
-        return pltpu.make_async_copy(src, ring.at[s, which], ring_sem.at[s, which])
-
-    def d_copy(g, which):
-        src = dw.at[:, pl.ds(pl.multiple_of((g * 2 + which) * CW, CW), CW)]
+        return pltpu.make_async_copy(src, ring.at[s, :, pl.ds(which * CW, CW)], ring_sem.at[s, which])
+
+    def d_copy(g):
+        src = dw.at[:, pl.ds(pl.multiple_of(g * 2 * CW, 2 * CW), 2 * CW)]
         s = (chunks + g) % RING
-        return pltpu.make_async_copy(src, ring.at[s, which, pl.ds(0, units)], ring_sem.at[s, which])
+        return pltpu.make_async_copy(src, ring.at[s, pl.ds(0, units)], ring_sem.at[s, 0])
 
     for c in range(min(RING, chunks)):
         gu_copy(c, 0).start()
@@ -121,66 +120,100 @@
 
                 cross_copy(z + t, h, False).start()
     keep.wait()
+
+    def part_copy(q):
+        return pltpu.make_async_remote_copy(
+            src_ref=part.at[q % KEEP, 1 - gx], dst_ref=precv.at[q],
+            send_sem=part_send.at[q % KEEP], recv_sem=part_recv.at[q],
+            device_id=core, device_id_type=MESH)
+
+    def hid_at(far, c, which):
+        at = pl.ds(pl.multiple_of(far * line + which * half, half), half)
+        return hid.at[at, pl.ds(pl.multiple_of(c * CW, CW), CW)]
+
+    def hid_copy(q, far, c, which):
+        return pltpu.make_async_remote_copy(
+            src_ref=hid_at(far, c, which), dst_ref=hid_at(far, c, which),
+            send_sem=hid_send.at[q], recv_sem=hid_recv.at[q],
+            device_id=core, device_id_type=MESH)
+
+    def finish(q, far, c):
+        part_copy(q).wait_recv()
+        both = part[q % KEEP, gx] + precv[q]
+        gate, up = both[:, :CW], both[:, CW:]
+        hid_at(far, c, gx)[...] = (gate / (1.0 + jnp.exp(-gate)) * up).astype(BF16)
+        hid_copy(q, far, c, gx).start()
+
+    def multiply(q, far, c):
+        @pl.when(q >= KEEP)
+        def _():
+            part_copy(q - KEEP).wait_send()
+
+        term = jnp.dot(x_all[far * line:(far + 1) * line], ring[c % RING], preferred_element_type=F32)
+        part[q % KEEP, 0] = term[:half]
+        part[q % KEEP, 1] = term[half:]
+        part_copy(q).start()
+
+    def arrive(c):
+        gu_copy(c, 0).wait()
+        gu_copy(c, 1).wait()
+
+    def refill(c):
+        nxt = c + RING
+
+        @pl.when(nxt < chunks)
+        def _():
+            gu_copy(nxt, 0).start()
+            gu_copy(nxt, 1).start()
+
+        @pl.when((nxt >= chunks) & (nxt < chunks + groups))
+        def _():
+            d_copy(nxt - chunks).start()
+
+    def near_step(c, carry):
+        arrive(c)
+        multiply(c, 0, c)
+
+        @pl.when(c >= 1)
+        def _():
+            finish(c - 1, 0, c - 1)
+        return carry
+
+    def far_step(c, carry):
+        q = RING + c
+        multiply(q, 1, c)
+        refill(c)
+
+        @pl.when(c == 0)
+        def _():
+            finish(RING - 1, 0, RING - 1)
+
+        @pl.when(c >= 1)
+        def _():
+            finish(q - 1, 1, c - 1)
+        return carry
+
+    def both_step(c, carry):
+        q = 2 * c
+        arrive(c)
+        multiply(q, 0, c)
+        finish(q - 1, 1, c - 1)
+        multiply(q + 1, 1, c)
+        refill(c)
+        finish(q, 0, c)
+        return carry
+
+    lax.fori_loop(0, RING, near_step, 0)
     for b in range(nz):
         for h in range(CUT):
             cross_copy(b, h, False).wait_recv()
-
-    def part_copy(c):
-        return pltpu.make_async_remote_copy(
-            src_ref=part.at[c % KEEP, 1 - gx], dst_ref=precv.at[c],
-            send_sem=part_send.at[c % KEEP], recv_sem=part_recv.at[c],
-            device_id=core, device_id_type=MESH)
-
-    def hid_at(c, which):
-        return hid.at[pl.ds(pl.multiple_of(which * half, half), half), pl.ds(pl.multiple_of(c * CW, CW), CW)]
-
-    def hid_copy(c, which):
-        return pltpu.make_async_remote_copy(
-            src_ref=hid_at(c, which), dst_ref=hid_at(c, which),
-            send_sem=hid_send.at[c], recv_sem=hid_recv.at[c],
-            device_id=core, device_id_type=MESH)
-
-    def finish(c):
-        part_copy(c).wait_recv()
-        gate = part[c % KEEP, gx, 0].astype(F32) + precv[c, 0].astype(F32)
-        up = part[c % KEEP, gx, 1].astype(F32) + precv[c, 1].astype(F32)
-        hid_at(c, gx)[...] = (gate / (1.0 + jnp.exp(-gate)) * up).astype(BF16)
-        hid_copy(c, gx).start()
-
-    def gu_step(c, carry):
-        s = c % RING
-
-        @pl.when(c >= KEEP)
-        def _():
-            part_copy(c - KEEP).wait_send()
-
-        for which in range(2):
-            gu_copy(c, which).wait()
-            term = jnp.dot(x_all[...], ring[s, which], preferred_element_type=F32)
-            part[c % KEEP, 0, which] = term[:half].astype(part.dtype)
-            part[c % KEEP, 1, which] = term[half:].astype(part.dtype)
-        part_copy(c).start()
-        nxt = c + RING
-
-        @pl.when(nxt < chunks)
-        def _():
-            gu_copy(nxt, 0).start()
-            gu_copy(nxt, 1).start()
-
-        @pl.when((nxt >= chunks) & (nxt < chunks + groups))
-        def _():
-            d_copy(nxt - chunks, 0).start()
-            d_copy(nxt - chunks, 1).start()
-
-        @pl.when(c >= 1)
-        def _():
-            finish(c - 1)
-        return carry
-
-    lax.fori_loop(0, chunks, gu_step, 0)
-    finish(chunks - 1)
-    for c in range(chunks):
-        hid_copy(c, 1 - gx).wait_recv()
+    lax.fori_loop(0, RING, far_step, 0)
+    lax.fori_loop(RING, chunks, both_step, 0)
+    finish(2 * chunks - 1, 1, chunks - 1)
+    order = [(0, c) for c in range(RING)] + [(1, c) for c in range(RING)]
+    order += [(far, c) for c in range(RING, chunks) for far in range(2)]
+    for q, (far, c) in enumerate(order):
+        hid_copy(q, far, c, 1 - gx).wait_recv()
 
     def x_copy(g):
         return pltpu.make_async_remote_copy(
@@ -197,7 +230,7 @@
         x_copy(g).wait_recv()
         for k in range(nz):
             at = pl.ds(pl.multiple_of(lax.rem(z + k, nz) * rows, rows), rows)
-            both = yown[g, :, at, :] + xrecv[g, :, at, :].astype(F32)
+            both = yown[g, at] + xrecv[g, at].astype(F32)
             if k == 0:
                 fin[g] = both
             else:
@@ -206,12 +239,11 @@
 
     def d_step(g, carry):
         s = (chunks + g) % RING
-        for which in range(2):
-            d_copy(g, which).wait()
-            y = jnp.dot(hid[...], ring[s, which, :units], preferred_element_type=F32)
-            yown[g, which] = y[:line]
-            xsend[g, which] = y[line:].astype(BF16)
+        d_copy(g).wait()
+        far = jnp.dot(hid[line:], ring[s, :units], preferred_element_type=F32)
+        xsend[g] = far.astype(BF16)
         x_copy(g).start()
+        yown[g] = jnp.dot(hid[:line], ring[s, :units], preferred_element_type=F32)
 
         @pl.when(g >= LAG)
         def _():
@@ -226,8 +258,7 @@
         for k in range(1, nz):
             z_copy(g, k).wait_recv()
             total = total + zrecv[k - 1, g].astype(F32)
-        for which in range(2):
-            out[:, pl.ds((g * 2 + which) * CW, CW)] = total[which].astype(BF16)
+        out[:, pl.ds(g * 2 * CW, 2 * CW)] = total.astype(BF16)
 
     for h in range(CUT):
         for b in range(nz):
@@ -240,10 +271,10 @@
             @pl.when((z > 0) & (b >= z))
             def _():
                 line_copy(b, h, False, -1, dn_send).wait_send()
-    for c in range(max(chunks - KEEP, 0), chunks):
-        part_copy(c).wait_send()
-    for c in range(chunks):
-        hid_copy(c, gx).wait_send()
+    for q, (far, c) in enumerate(order):
+        if q >= len(order) - KEEP:
+            part_copy(q).wait_send()
+        hid_copy(q, far, c, gx).wait_send()
     for g in range(groups):
         x_copy(g).wait_send()
         for k in range(1, nz):
@@ -263,17 +294,17 @@
         in_specs=[pl.BlockSpec(memory_space=pl.ANY)] * 4,
         out_specs=pl.BlockSpec(memory_space=pltpu.VMEM),
         scratch_shapes=[
-            pltpu.VMEM((RING, 2, depth, CW), BF16),
+            pltpu.VMEM((RING, depth, 2 * CW), BF16),
             pltpu.VMEM((2 * line, depth), BF16),
             pltpu.VMEM((2 * line, units), BF16),
-            pltpu.VMEM((KEEP, 2, 2, line, CW), EX),
-            pltpu.VMEM((chunks, 2, line, CW), EX),
-            pltpu.VMEM((groups, 2, line, CW), F32),
-            pltpu.VMEM((groups, 2, line, CW), BF16),
-            pltpu.VMEM((groups, 2, line, CW), BF16),
-            pltpu.VMEM((nz - 1, groups, 2, rows, CW), BF16),
-            pltpu.VMEM((nz - 1, groups, 2, rows, CW), BF16),
-            pltpu.VMEM((groups, 2, rows, CW), F32),
+            pltpu.VMEM((KEEP, 2, line // 2, 2 * CW), F32),
+            pltpu.VMEM((2 * chunks, line // 2, 2 * CW), F32),
+            pltpu.VMEM((groups, line, 2 * CW), F32),
+            pltpu.VMEM((groups, line, 2 * CW), BF16),
+            pltpu.VMEM((groups, line, 2 * CW), BF16),
+            pltpu.VMEM((nz - 1, groups, rows, 2 * CW), BF16),
+            pltpu.VMEM((nz - 1, groups, rows, 2 * CW), BF16),
+            pltpu.VMEM((groups, rows, 2 * CW), F32),
             dma((RING, 2)),
             dma,
             dma((nz, CUT)),
@@ -282,9 +313,9 @@
             dma((nz, CUT)),
             dma((nz, CUT)),
             dma((KEEP,)),
-            dma((chunks,)),
-            dma((chunks,)),
-            dma((chunks,)),
+            dma((2 * chunks,)),
+            dma((2 * chunks,)),
+            dma((2 * chunks,)),
             dma((groups,)),
             dma((groups,)),
             dma((nz - 1, groups)),

time: 98.3 us -> 82.4 us (0.84)
  Pallas kernels: 96.5 us -> 80.6 us
    pallas_call x1, Pallas kernels: 96.5 us -> 80.6 us  [fused(): pl.pallas_call(functools.partial(kernel, rows, width, units, nz), out_sha...]
where the time goes in v2:
time: 82.4 us; the launch traced here: 82.2 us
  Pallas kernels  80.6 us (98%)
  local copies, waits for them, and re-layouts  1.67 us (2%)
    pallas_call x1, Pallas kernels, fused(): pl.pallas_call(functools.partial(kernel, rows, width, units, nz), out_sha...  80.6 us
    unnamed x1, local copies, waits for them, and re-layouts  1.67 us

profile of v2, /device:TPU:0, one launch (start us, length us, event | category | flops | bytes accessed | tf_op | source)
XLA Modules:
  0.0 82.2 jit_solution(16540811334461757899)
XLA Ops:
  0.0 80.6 %shard_map.46 = bf16[32,4096]{1,0:T(8,128)(2,1)} custom-call(bf16[32,4096]{1,0:T(8,128)(2,1)} %tok.1, bf16[4096,3328]{1,0:T(8,128)(2,1)} %gw.1, bf16[4096,3328]{1,0:T(8,128)(2,1)} %uw.1, bf16[3328,4096]{1,0:T(8,128)(2,1)} %dw.1), custom_call_target="tpu_custom_call" | custom-call | flops 20937965568 | bytes 81788928 | tf_op jit(solution)/shard_map/pallas_call | solution.py:291
  80.6 1.7 %copy.6 = bf16[32,4096]{1,0:T(8,128)(2,1)} copy(bf16[32,4096]{1,0:T(8,128)(2,1)} %shard_map.46) | data formatting | bytes 524288

commit v3 on v2

--- a/solution.py
+++ b/solution.py
@@ -11,9 +11,10 @@
 MESH = pl.DeviceIdType.MESH
 CW = 256
 RING = 10
-KEEP = 4
+KEEP = 6
+BEHIND = 3
 LAG = 2
-CUT = 2
+CUT = 4
 
 
 def local(tokens, gate_weight, up_weight, down_weight):
@@ -66,13 +67,13 @@
         pl.semaphore_signal(barrier, inc=1, device_id=along(lax.rem(z + k, nz)), device_id_type=MESH)
     pl.semaphore_wait(barrier, nz + 1)
 
-    cut = rows // CUT
+    cut = tok.shape[1] // CUT
 
     def place(block, h, far):
-        return x_all.at[pl.ds(pl.multiple_of(far * line + block * rows + h * cut, cut), cut)]
+        return x_all.at[pl.ds(pl.multiple_of(far * line + block * rows, rows), rows), pl.ds(h * cut, cut)]
 
     def source(block, h, own):
-        return tok.at[pl.ds(h * cut, cut)] if own else place(block, h, 0)
+        return tok.at[:, pl.ds(h * cut, cut)] if own else place(block, h, 0)
 
     def line_copy(block, h, own, step, sems):
         return pltpu.make_async_remote_copy(
@@ -137,22 +138,23 @@
             send_sem=hid_send.at[q], recv_sem=hid_recv.at[q],
             device_id=core, device_id_type=MESH)
 
-    def finish(q, far, c):
-        part_copy(q).wait_recv()
-        both = part[q % KEEP, gx] + precv[q]
-        gate, up = both[:, :CW], both[:, CW:]
-        hid_at(far, c, gx)[...] = (gate / (1.0 + jnp.exp(-gate)) * up).astype(BF16)
-        hid_copy(q, far, c, gx).start()
-
-    def multiply(q, far, c):
+    def step(q, far, c, done):
         @pl.when(q >= KEEP)
         def _():
             part_copy(q - KEEP).wait_send()
 
-        term = jnp.dot(x_all[far * line:(far + 1) * line], ring[c % RING], preferred_element_type=F32)
-        part[q % KEEP, 0] = term[:half]
-        part[q % KEEP, 1] = term[half:]
-        part_copy(q).start()
+        if done is not None:
+            part_copy(done[0]).wait_recv()
+            both = part[done[0] % KEEP, gx] + precv[done[0]]
+            gate, up = both[:, :CW], both[:, CW:]
+            hid_at(*done[1:], gx)[...] = (gate / (1.0 + jnp.exp(-gate)) * up).astype(BF16)
+        if c is not None:
+            term = jnp.dot(x_all[far * line:(far + 1) * line], ring[c % RING], preferred_element_type=F32)
+            part[q % KEEP, 0] = term[:half]
+            part[q % KEEP, 1] = term[half:]
+            part_copy(q).start()
+        if done is not None:
+            hid_copy(*done, gx).start()
 
     def arrive(c):
         gu_copy(c, 0).wait()
@@ -172,46 +174,38 @@
 
     def near_step(c, carry):
         arrive(c)
-        multiply(c, 0, c)
-
-        @pl.when(c >= 1)
-        def _():
-            finish(c - 1, 0, c - 1)
+        step(c, 0, c, (c - BEHIND, 0, c - BEHIND))
         return carry
 
     def far_step(c, carry):
-        q = RING + c
-        multiply(q, 1, c)
+        step(RING + c, 1, c, (RING + c - BEHIND, 1, c - BEHIND))
         refill(c)
-
-        @pl.when(c == 0)
-        def _():
-            finish(RING - 1, 0, RING - 1)
-
-        @pl.when(c >= 1)
-        def _():
-            finish(q - 1, 1, c - 1)
         return carry
 
-    def both_step(c, carry):
-        q = 2 * c
+    order = [(0, c) for c in range(RING)] + [(1, c) for c in range(RING)]
+    order += [(far, c) for c in range(RING, chunks) for far in range(2)]
+
+    def before(q):
+        return (q - BEHIND,) + order[q - BEHIND]
+
+    for c in range(BEHIND):
         arrive(c)
-        multiply(q, 0, c)
-        finish(q - 1, 1, c - 1)
-        multiply(q + 1, 1, c)
-        refill(c)
-        finish(q, 0, c)
-        return carry
-
-    lax.fori_loop(0, RING, near_step, 0)
+        step(c, 0, c, None)
+    lax.fori_loop(BEHIND, RING, near_step, 0)
     for b in range(nz):
         for h in range(CUT):
             cross_copy(b, h, False).wait_recv()
-    lax.fori_loop(0, RING, far_step, 0)
-    lax.fori_loop(RING, chunks, both_step, 0)
-    finish(2 * chunks - 1, 1, chunks - 1)
-    order = [(0, c) for c in range(RING)] + [(1, c) for c in range(RING)]
-    order += [(far, c) for c in range(RING, chunks) for far in range(2)]
+    for c in range(BEHIND):
+        step(RING + c, 1, c, before(RING + c))
+        refill(c)
+    lax.fori_loop(BEHIND, RING, far_step, 0)
+    for c in range(RING, chunks):
+        arrive(c)
+        step(2 * c, 0, c, before(2 * c))
+        step(2 * c + 1, 1, c, before(2 * c + 1))
+        refill(c)
+    for q in range(2 * chunks, 2 * chunks + BEHIND):
+        step(q, 0, None, before(q))
     for q, (far, c) in enumerate(order):
         hid_copy(q, far, c, 1 - gx).wait_recv()
 
@@ -272,7 +266,7 @@
             def _():
                 line_copy(b, h, False, -1, dn_send).wait_send()
     for q, (far, c) in enumerate(order):
-        if q >= len(order) - KEEP:
+        if q >= len(order) + BEHIND - KEEP:
             part_copy(q).wait_send()
         hid_copy(q, far, c, gx).wait_send()
     for g in range(groups):
@@ -339,7 +333,7 @@
         units, width = down_weight.shape
         fits = gy == 8 and gx == 2 and rows == 32 and units % CW == 0 and width % (2 * CW) == 0
         fits = fits and units <= depth == width <= 4096
-        fits = fits and RING >= width // (2 * CW) and units // CW >= KEEP
+        fits = fits and RING >= width // (2 * CW) and RING > BEHIND
         fits = fits and RING <= units // CW and units <= 3328
         if fits:
             return fused(gy // 2, tokens, gate_weight, up_weight, down_weight)

time: 82.4 us -> 78.3 us (0.950)
  Pallas kernels: 80.6 us -> 76.5 us
    pallas_call x1, Pallas kernels: 80.6 us -> 76.5 us  [fused(): pl.pallas_call(functools.partial(kernel, rows, width, units, nz), out_sha...]
where the time goes in v3:
time: 78.3 us; the launch traced here: 78.2 us
  Pallas kernels  76.5 us (98%)
  local copies, waits for them, and re-layouts  1.67 us (2%)
    pallas_call x1, Pallas kernels, fused(): pl.pallas_call(functools.partial(kernel, rows, width, units, nz), out_sha...  76.5 us
    unnamed x1, local copies, waits for them, and re-layouts  1.67 us

profile of v3, /device:TPU:0, one launch (start us, length us, event | category | flops | bytes accessed | tf_op | source)
XLA Modules:
  0.0 78.2 jit_solution(12907074225763454142)
XLA Ops:
  0.0 76.5 %shard_map.46 = bf16[32,4096]{1,0:T(8,128)(2,1)} custom-call(bf16[32,4096]{1,0:T(8,128)(2,1)} %tok.1, bf16[4096,3328]{1,0:T(8,128)(2,1)} %gw.1, bf16[4096,3328]{1,0:T(8,128)(2,1)} %uw.1, bf16[3328,4096]{1,0:T(8,128)(2,1)} %dw.1), custom_call_target="tpu_custom_call" | custom-call | flops 20937965568 | bytes 81788928 | tf_op jit(solution)/shard_map/pallas_call | solution.py:285
  76.5 1.7 %copy.6 = bf16[32,4096]{1,0:T(8,128)(2,1)} copy(bf16[32,4096]{1,0:T(8,128)(2,1)} %shard_map.46) | data formatting | bytes 524288
